TPU v7x, 32 devices: a whole 2x2x4 slice. The times are simulated.
32 devices in a mesh: branch: 2 (over core), seq: 8 (over z, y), mp: 2 (over x).
Axes of the slice: x: 2, y: 2, z: 4, core: 2. Of those that a mesh axis runs over, the one named last changes fastest.
Arguments:
- tokens: bfloat16 [2048, 4096], P('seq', 'mp'), may hold values from -6 to 6
- light_in: bfloat16 [4096, 2048], P(None, ('branch', 'mp')), may hold values from -0.09375 to 0.09375
- light_out: bfloat16 [2048, 4096], P(('branch', 'mp')), may hold values from -0.1875 to 0.1875
- heavy_in: bfloat16 [4096, 16384], P(None, ('branch', 'seq', 'mp')), may hold values from -0.09375 to 0.09375
- heavy_out: bfloat16 [16384, 4096], P(('branch', 'seq', 'mp')), may hold values from -0.09375 to 0.09375
- route_index: int32 [8, 32], P('seq'), may hold values from 0 to 255, as said below
- route_count: int32 [8], P('seq'), may hold values from 1 to 32, as said below
- route_gate: float32 [8, 32], P('seq'), may hold values from 0.25 to 2
- cotangent: bfloat16 [2048, 4096], P('seq', 'mp'), may hold values from -6 to 6
Outputs:
- mixed: bfloat16 [2048, 4096], P('seq', ('branch', 'mp'))
- grad_heavy_in: bfloat16 [4096, 16384], P(None, ('branch', 'seq', 'mp'))
- grad_heavy_out: bfloat16 [16384, 4096], P(('branch', 'seq', 'mp'))
Inputs may be any that keep to these rules, and one draw needn't show every extreme that they name: `route_index`: each row holds 32 distinct positions of its shard. The first route_count[s] slots of shard s are live; some shard has all 32 slots live.
All inputs are finite; a program needn't handle non-finite values.
Results may differ from a plain program's by a relative error of at most 0.008.
Values may be sent and summed in bfloat16 or wider, within the bound.
A program may use at most 128 MiB of HBM per device.

v0:
```python
import jax
import jax.numpy as jnp
from jax import lax
from jax.sharding import PartitionSpec as P

root_coef = 0.7978845608
cubic_coef = 0.044715


def gelu_tanh(values):
    inner = root_coef * (values + cubic_coef * values * values * values)
    return 0.5 * values * (1.0 + jnp.tanh(inner))


def gelu_slope(values):
    tangent = jnp.tanh(root_coef * (values + cubic_coef * values * values * values))
    return 0.5 * (1.0 + tangent) + 0.5 * values * (1.0 - tangent * tangent) * root_coef * (
        1.0 + 3.0 * cubic_coef * values * values
    )


def over_rows(left, right):
    return lax.dot_general(
        left, right, (((0,), (0,)), ((), ())), preferred_element_type=jnp.float32
    )


def over_cols(left, right):
    return lax.dot_general(
        left, right, (((1,), (1,)), ((), ())), preferred_element_type=jnp.float32
    )


def per_device(
    tokens,
    light_in,
    light_out,
    heavy_in,
    heavy_out,
    route_index,
    route_count,
    route_gate,
    cotangent,
):
    whole = lax.all_gather(tokens, "mp", axis=1, tiled=True)
    light_hidden = gelu_tanh(jnp.dot(whole, light_in, preferred_element_type=jnp.float32)).astype(
        jnp.bfloat16
    )
    light_terms = jnp.dot(light_hidden, light_out, preferred_element_type=jnp.float32)
    light_share = lax.psum_scatter(light_terms, ("branch", "mp"), scatter_dimension=1, tiled=True)
    positions = route_index[0]
    slot_count = route_index.shape[1]
    live_slots = jnp.arange(slot_count, dtype=jnp.int32) < route_count[0]
    row_scale = jnp.where(live_slots, route_gate[0], jnp.zeros_like(route_gate[0]))
    picked = jnp.take(tokens, positions, axis=0)
    back_rows = (
        jnp.take(cotangent, positions, axis=0).astype(jnp.float32) * row_scale[:, None]
    ).astype(jnp.bfloat16)
    picked, back_rows = (
        lax.all_gather(picked, "mp", axis=1, tiled=True),
        lax.all_gather(back_rows, "mp", axis=1, tiled=True),
    )
    picked, back_rows = (
        lax.all_gather(picked, "seq", axis=0, tiled=True),
        lax.all_gather(back_rows, "seq", axis=0, tiled=True),
    )
    pre_act = jnp.dot(picked, heavy_in, preferred_element_type=jnp.float32)
    heavy_hidden = gelu_tanh(pre_act).astype(jnp.bfloat16)
    grad_out = over_rows(heavy_hidden, back_rows).astype(jnp.bfloat16)
    slope = (over_cols(back_rows, heavy_out) * gelu_slope(pre_act)).astype(jnp.bfloat16)
    grad_in = over_rows(picked, slope).astype(jnp.bfloat16)
    partial_terms = jnp.dot(heavy_hidden, heavy_out, preferred_element_type=jnp.float32)
    homed = lax.psum_scatter(
        partial_terms.astype(jnp.bfloat16), "seq", scatter_dimension=0, tiled=True
    ).astype(jnp.float32)
    homed = lax.psum_scatter(
        homed.astype(jnp.bfloat16), ("branch", "mp"), scatter_dimension=1, tiled=True
    ).astype(jnp.float32)
    heavy_share = homed * row_scale[:, None]
    mixed = light_share.at[positions].add(heavy_share).astype(jnp.bfloat16)
    return (mixed, grad_in, grad_out)


def solution(mesh):
    in_specs = (
        P("seq", "mp"),
        P(None, ("branch", "mp")),
        P(("branch", "mp"), None),
        P(None, ("branch", "seq", "mp")),
        P(("branch", "seq", "mp"), None),
        P("seq", None),
        P("seq"),
        P("seq", None),
        P("seq", "mp"),
    )
    out_specs = (
        P("seq", ("branch", "mp")),
        P(None, ("branch", "seq", "mp")),
        P(("branch", "seq", "mp"), None),
    )
    return jax.shard_map(
        per_device, mesh=mesh, in_specs=in_specs, out_specs=out_specs, check_vma=False
    )
```

profile of v0, /device:TPU:0, one launch (start us, length us, event | category | flops | bytes accessed | tf_op | source)
XLA Modules:
  0.0 226.3 jit_solution(11586134781941568956)
XLA Ops:
  8.0 0.0 copy-start
  8.0 0.0 all-gather.6.cloned.1.call-start
  8.1 0.7 compare_select_fusion
  8.8 0.7 compare_and_fusion
  9.5 2.1 gather_fusion
  11.6 0.1 broadcast_select_fusion
  11.7 7.2 %all_gather.16 = bf16[32,4096]{1,0:T(8,128)(2,1)} all-gather(bf16[32,2048]{1,0:T(8,128)(2,1)S(1)} %broadcast_select_fusion), channel_id=1, replica_groups=mesh['branch'=2,'seq'=8,'mp'=2] {'mp'}, dimensions={1}, use_global_device_ids=true | all-gather | bytes 393216 | tf_op jit(solution)/shard_map/all_gather | solution.py:60
  18.9 0.0 all-gather.6.cloned.1.call-update
  18.9 0.0 reduce-scatter.6.cloned.1.call-start
  19.0 50.9 %all-gather.6.cloned.1.call-done = bf16[256,4096]{1,0:T(8,128)(2,1)} async-done(((bf16[32,4096]{1,0:T(8,128)(2,1)}), bf16[256,4096]{1,0:T(8,128)(2,1)}) %all-gather.6.cloned.1.call-update) | async-done | bytes 2097168 | tf_op jit(solution)/shard_map/all_gather | solution.py:64
  69.9 0.0 copy-start.3
  69.9 4.2 %fusion.47 = f32[256,512]{1,0:T(8,128)S(1)} fusion(bf16[256,4096]{1,0:T(8,128)(2,1)} %all-gather.6.cloned.1.call-done, bf16[4096,512]{1,0:T(8,128)(2,1)} %param.14), kind=kOutput, calls=%fused_computation.61 | convolution fusion | flops 1073741824 | bytes 6815744 | tf_op jit(solution)/shard_map/dot_general | solution.py:67
  74.1 0.0 copy-start.2
  74.1 0.8 copy-done.2
  74.9 0.0 copy-done.3
  74.9 2.7 %convolution_convert_fusion.2 = bf16[256,4096]{1,0:T(8,128)(2,1)} fusion(bf16[512,4096]{1,0:T(8,128)(2,1)S(1)} %copy-done.3, f32[256,512]{1,0:T(8,128)S(1)} %fusion.47), kind=kOutput, calls=%fused_computation.5 | convolution fusion | flops 1075970048 | bytes 6815744 | tf_op jit(solution)/shard_map/dot_general | solution.py:72
  77.5 0.0 copy-start.4
  77.5 0.0 reduce-scatter.6.cloned.1.call-update
  77.6 0.0 all-gather.4.cloned.1.call-start
  77.6 0.5 all-gather.4.cloned.1.call-update
  78.2 0.0 all-gather.8.cloned.1.call-start
  78.8 0.0 copy-done
  78.9 0.7 gather_fusion.1
  79.5 0.0 copy-done.4
  79.5 0.1 multiply_convert_fusion.1
  79.6 5.8 %all_gather.18 = bf16[32,4096]{1,0:T(8,128)(2,1)} all-gather(bf16[32,2048]{1,0:T(8,128)(2,1)S(1)} %multiply_convert_fusion.1), channel_id=1, replica_groups=mesh['branch'=2,'seq'=8,'mp'=2] {'mp'}, dimensions={1}, use_global_device_ids=true | all-gather | bytes 393216 | tf_op jit(solution)/shard_map/all_gather | solution.py:61
  85.4 0.0 all-gather.8.cloned.1.call-update
  85.4 0.0 reduce-scatter.8.cloned.1.call-start
  85.5 59.5 %reduce-scatter.6.cloned.1.call-done = bf16[32,4096]{1,0:T(8,128)(2,1)} async-done(((bf16[256,4096]{1,0:T(8,128)(2,1)}), bf16[32,4096]{1,0:T(8,128)(2,1)}) %reduce-scatter.6.cloned.1.call-update) | async-done | bytes 262160 | tf_op jit(solution)/shard_map/reduce_scatter | solution.py:73
  145.0 0.0 reduce-scatter.8.cloned.1.call-update
  145.0 0.0 reduce-scatter.4.cloned.1.call-start
  145.0 0.0 all-gather.4.cloned.1.call-done
  145.1 8.6 %fusion.20 = f32[256,4096]{1,0:T(8,128)} fusion(bf16[512,4096]{1,0:T(8,128)(2,1)} %param.13, bf16[256,4096]{1,0:T(8,128)(2,1)} %all-gather.4.cloned.1.call-done, bf16[4096,512]{1,0:T(8,128)(2,1)} %param.12), kind=kOutput, calls=%fused_computation.29 | convolution fusion | flops 2148663296 | bytes 14680064 | tf_op jit(solution)/shard_map/dot_general | solution.py:49
  153.6 0.0 copy-start.5
  153.6 0.0 reduce-scatter.4.cloned.1.call-update
  153.6 0.6 copy-done.5
  154.3 11.2 %all-gather.8.cloned.1.call-done = bf16[256,4096]{1,0:T(8,128)(2,1)} async-done(((bf16[32,4096]{1,0:T(8,128)(2,1)}), bf16[256,4096]{1,0:T(8,128)(2,1)}) %all-gather.8.cloned.1.call-update) | async-done | bytes 2097168 | tf_op jit(solution)/shard_map/all_gather | solution.py:65
  165.5 0.0 copy-start.1
  165.5 5.3 %convolution_convert_fusion = bf16[512,4096]{1,0:T(8,128)(2,1)} fusion(bf16[256,4096]{1,0:T(8,128)(2,1)} %all-gather.8.cloned.1.call-done, f32[256,512]{1,0:T(8,128)} %copy-done.2), kind=kOutput, calls=%fused_computation.3 | convolution fusion | flops 1077018624 | bytes 6815744 | tf_op jit(solution)/shard_map/dot_general | solution.py:23
  170.8 0.0 copy-done.1
  170.8 7.9 %convolution_convert_fusion.1 = bf16[4096,512]{1,0:T(8,128)(2,1)} fusion(bf16[256,4096]{1,0:T(8,128)(2,1)} %all-gather.6.cloned.1.call-done, bf16[256,4096]{1,0:T(8,128)(2,1)S(1)} %copy-done.1, bf16[512,4096]{1,0:T(8,128)(2,1)} %param.15, f32[256,512]{1,0:T(8,128)} %copy-done.2), kind=kOutput, calls=%fused_computation.4 | convolution fusion | flops 2152071168 | bytes 13107200 | tf_op jit(solution)/shard_map/dot_general | solution.py:23
  178.7 0.0 reduce-scatter.8.cloned.1.call-done
  178.7 34.9 %reduce-scatter.4.cloned.1.call-done = f32[256,1024]{1,0:T(8,128)} async-done(((f32[256,4096]{1,0:T(8,128)}), f32[256,1024]{1,0:T(8,128)}) %reduce-scatter.4.cloned.1.call-update) | async-done | bytes 1048592 | tf_op jit(solution)/shard_map/reduce_scatter | solution.py:50
  213.6 3.5 %scatter_custom_fusion = f32[256,1024]{1,0:T(8,128)} fusion(f32[256,1024]{1,0:T(8,128)} %reduce-scatter.4.cloned.1.call-done, s32[32]{0:T(128)S(1)} %fusion.35, bf16[32,1024]{1,0:T(8,128)(2,1)} %reduce-scatter.8.cloned.1.call-done, f32[32]{0:T(128)S(1)} %compare_select_fusion.2), kind=kCustom, calls=%fused_computation.40 | custom fusion | flops 98304 | bytes 1114624 | tf_op jit(solution)/shard_map/scatter-add | solution.py:80
  217.1 2.1 convert_element_type.36
  (3 shorter events, 0.0 us)
Async XLA Ops:
  8.0 70.9 %copy-start = (bf16[256,2048]{1,0:T(8,128)(2,1)S(1)}, bf16[256,2048]{1,0:T(8,128)(2,1)}, u32[]{:S(2)}) copy-start(bf16[256,2048]{1,0:T(8,128)(2,1)} %param.19) | copy-start | bytes 3145732
  8.0 61.9 %all-gather.6.cloned.1.call-start = ((), (), s32[]{:S(2)}) async-start(), calls=%async_computation.5 | async-start | bytes 2359296 | tf_op jit(solution)/shard_map/all_gather | solution.py:64
  18.9 126.1 %reduce-scatter.6.cloned.1.call-start = ((), (), s32[]{:S(2)}) async-start(), calls=%async_computation.6 | async-start | bytes 2359296 | tf_op jit(solution)/shard_map/reduce_scatter | solution.py:73
  69.9 5.0 %copy-start.3 = (bf16[512,4096]{1,0:T(8,128)(2,1)S(1)}, bf16[512,4096]{1,0:T(8,128)(2,1)}, u32[]{:S(2)}) copy-start(bf16[512,4096]{1,0:T(8,128)(2,1)} %param.15) | copy-start | bytes 12582916
  74.1 0.8 copy-start.2
  77.5 2.0 copy-start.4
  77.6 67.5 %all-gather.4.cloned.1.call-start = ((), (), s32[]{:S(2)}) async-start(), calls=%async_computation.3 | async-start | bytes 3145728 | tf_op jit(solution)/shard_map/all_gather | solution.py:45
  78.2 87.3 %all-gather.8.cloned.1.call-start = ((), (), s32[]{:S(2)}) async-start(), calls=%async_computation.8 | async-start | bytes 2359296 | tf_op jit(solution)/shard_map/all_gather | solution.py:65
  85.4 93.3 %reduce-scatter.8.cloned.1.call-start = ((), (), s32[]{:S(2)}) async-start(), calls=%async_computation.7 | async-start | bytes 327680 | tf_op jit(solution)/shard_map/reduce_scatter | solution.py:76
  145.0 68.7 %reduce-scatter.4.cloned.1.call-start = ((), (), s32[]{:S(2)}) async-start(), calls=%async_computation.4 | async-start | bytes 5242880 | tf_op jit(solution)/shard_map/reduce_scatter | solution.py:50
  153.6 0.7 copy-start.5
  165.5 5.3 %copy-start.1 = (bf16[256,4096]{1,0:T(8,128)(2,1)S(1)}, bf16[256,4096]{1,0:T(8,128)(2,1)}, u32[]{:S(2)}) copy-start(bf16[256,4096]{1,0:T(8,128)(2,1)} %all-gather.8.cloned.1.call-done) | copy-start | bytes 6291460
Sparse Core Ops, SparseCore 0:
  19.0 50.8 all-gather.5
  77.7 67.2 reduce-scatter.5
  147.4 19.0 reduce-scatter.7
  169.1 44.5 reduce-scatter.3
Sparse Core Ops, SparseCore 1:
  79.7 31.4 all-gather.3
  113.1 52.3 all-gather.7
where the time goes:
time: 227 us; the launch traced here: 226 us
  waiting for transfers between devices  157 us (69%)
  matrix products  28.6 us (13%)
  between operations  15.9 us (7%)
  blocking collectives  12.9 us (6%)
  other arithmetic  7.14 us (3%)
  local copies, waits for them, and re-layouts  4.22 us (2%)
    reduce_scatter x1, waiting for transfers between devices, per_device(): lax.psum_scatter(partial_terms.astype(jnp.bfloat16), 'seq', scatter_dimen...  59.5 us
    all_gather x1, waiting for transfers between devices, per_device(): lax.all_gather(picked, 'seq', axis=0, tiled=True)  50.9 us
    reduce_scatter x1, waiting for transfers between devices, per_device(): lax.psum_scatter(light_terms, ('branch', 'mp'), scatter_dimension=1, tile...  34.9 us
    dot_general x2, matrix products, over_rows(): lax.dot_general(left, right, (((0,), (0,)), ((), ())), preferred_element_...  13.2 us
    all_gather x1, waiting for transfers between devices, per_device(): lax.all_gather(back_rows, 'seq', axis=0, tiled=True)  11.2 us
    dot_general x1, matrix products, per_device(): jnp.dot(light_hidden, light_out, preferred_element_type=jnp.float32)  8.55 us
    all_gather x1, blocking collectives, per_device(): lax.all_gather(picked, 'mp', axis=1, tiled=True)  7.19 us
    all_gather x1, blocking collectives, per_device(): lax.all_gather(back_rows, 'mp', axis=1, tiled=True)  5.75 us
  transfers between devices with their start and end apart: 6, of which 4 were waited for; matrix products, arithmetic and copies ran while one was open for 10% of the time, Pallas kernels for 0%

commit v1 on v0

v1 whole, which is shorter than its diff:
```python
import functools

import jax
import jax.numpy as jnp
from jax import lax
from jax.experimental import pallas as pl
from jax.experimental.pallas import tpu as pltpu
from jax.sharding import PartitionSpec as P

root_coef = 0.7978845608
cubic_coef = 0.044715
MESH = pl.DeviceIdType.MESH
F32 = jnp.float32
BF16 = jnp.bfloat16


def gelu_both(values):
    square = values * values
    tangent = jnp.tanh(root_coef * (values + cubic_coef * square * values))
    half = 0.5 * (1.0 + tangent)
    slope = half + 0.5 * values * (1.0 - tangent * tangent) * root_coef * (
        1.0 + 3.0 * cubic_coef * square
    )
    return values * half, slope


def gelu_tanh(values):
    return gelu_both(values)[0]


def over_rows(left, right):
    return lax.dot_general(left, right, (((0,), (0,)), ((), ())), preferred_element_type=F32)


def over_cols(left, right):
    return lax.dot_general(left, right, (((1,), (1,)), ((), ())), preferred_element_type=F32)


def dot(left, right):
    return jnp.dot(left, right, preferred_element_type=F32)


def tile_of(size, most):
    tile = min(size, most)
    while size % tile:
        tile //= 2
    return tile


def kernel(
    n_seq,
    sizes,
    tokens,
    light_in,
    light_out,
    heavy_in,
    heavy_out,
    index,
    count,
    gate,
    cotangent,
    mixed,
    rows_out,
    hidden,
    slope,
    whole,
    cot,
    w_lin,
    w_lout,
    w_hin,
    w_hout,
    rows_all,
    l_hidden,
    l_own,
    l_send,
    l_recv,
    l_xsend,
    l_xrecv,
    h_slope,
    h_own,
    h_send,
    h_recv,
    y_send,
    y_recv,
    z_send,
    z_recv,
    x_send,
    x_recv,
    local_sem,
    send_sem,
    recv_sem,
):
    tok, half_d, ffl, ffh, cap = sizes
    width = 2 * half_d
    out_w = width // 4
    n_hi = n_seq // 2
    part = cap // 2
    total_rows = n_seq * cap
    b = lax.axis_index("branch")
    s = lax.axis_index("seq")
    m = lax.axis_index("mp")
    hi, lo = s // 2, s % 2
    sibling = {"branch": 1 - b}
    across = {"mp": 1 - m}
    beside = {"seq": hi * 2 + (1 - lo)}

    def hi_plus(d):
        return lax.rem(hi + d, n_hi)

    def hi_less(d):
        return lax.rem(hi + (n_hi - d), n_hi)

    local = []

    def load(src, dst):
        copy = pltpu.make_async_copy(src, dst, local_sem.at[len(local)])
        copy.start()
        local.append(copy)
        return copy

    own_cols = pl.ds(pl.multiple_of(m * half_d, half_d), half_d)
    load_tok = load(tokens, whole.at[:, own_cols])
    load_cot = load(cotangent, cot)
    load_lin = load(light_in, w_lin)
    load_lout = load(light_out, w_lout)
    load_hin = load(heavy_in, w_hin)
    load_hout = load(heavy_out, w_hout)

    barrier = pltpu.get_barrier_semaphore()
    peers = [sibling, across, beside] + [{"seq": hi_plus(d) * 2 + lo} for d in range(1, n_hi)]
    for peer in peers:
        pl.semaphore_signal(barrier, inc=1, device_id=peer, device_id_type=MESH)

    names = index[...].astype(F32)
    live = lax.broadcasted_iota(jnp.int32, (1, cap), 1) < count[0]
    scale_row = jnp.where(live, gate[...], 0.0)

    def column_of(row, first, rows):
        at = lax.broadcasted_iota(jnp.int32, (rows, cap), 0) + first
        to = lax.broadcasted_iota(jnp.int32, (rows, cap), 1)
        spread = jnp.where(at == to, jnp.broadcast_to(row, (rows, cap)), 0.0)
        return jnp.sum(spread, axis=1, keepdims=True)

    names_col = column_of(names, b * part, part)
    scale_part = column_of(scale_row, b * part, part)
    choose = jnp.where(
        lax.broadcasted_iota(jnp.int32, (part, tok), 1).astype(F32) == names_col, 1.0, 0.0
    ).astype(BF16)

    def rows_of(hi_at, lo_at, half):
        return pl.ds(pl.multiple_of((hi_at * 2 + lo_at) * cap + half * part, part), part)

    mine = rows_of(hi, lo, b)
    load_tok.wait()
    rows_all[0, mine, own_cols] = dot(choose, whole[:, own_cols]).astype(BF16)
    load_cot.wait()
    rows_all[1, mine, own_cols] = (dot(choose, cot[...]) * scale_part).astype(BF16)

    pl.semaphore_wait(barrier, len(peers))

    keys = {}
    sends = []

    def key_of(key):
        return keys.setdefault(key, len(keys))

    def send(key, src, dst, device):
        at = key_of(key)
        copy = pltpu.make_async_remote_copy(
            src_ref=src,
            dst_ref=dst,
            send_sem=send_sem.at[at],
            recv_sem=recv_sem.at[at],
            device_id=device,
            device_id_type=MESH,
        )
        copy.start()
        sends.append(copy)

    def arrive(key, dst, device):
        at = key_of(key)
        pltpu.make_async_remote_copy(
            src_ref=dst,
            dst_ref=dst,
            send_sem=send_sem.at[at],
            recv_sem=recv_sem.at[at],
            device_id=device,
            device_id_type=MESH,
        ).wait_recv()

    other_cols = pl.ds(pl.multiple_of((1 - m) * half_d, half_d), half_d)
    for k in range(2):
        view = rows_all.at[k, mine, own_cols]
        send(("x", k), view, view, across)
    tok_half = tok // 2
    my_tok = pl.ds(pl.multiple_of(b * tok_half, tok_half), tok_half)
    its_tok = pl.ds(pl.multiple_of((1 - b) * tok_half, tok_half), tok_half)
    send("tok", tokens.at[my_tok], whole.at[my_tok, own_cols], across)

    for k in range(2):
        arrive(("x", k), rows_all.at[k, mine, other_cols], across)
        view = rows_all.at[k, mine]
        for d in range(1, n_hi):
            send(("z", k, d), view, view, {"seq": hi_plus(d) * 2 + lo})
        send(("y", k, 0), view, view, beside)
        send(("s", k, 0, 0), view, view, sibling)

    def from_z(k):
        for d in range(1, n_hi):
            view = rows_all.at[k, rows_of(hi_less(d), lo, b)]
            arrive(("z", k, d), view, {"seq": hi_less(d) * 2 + lo})
            send(("y", k, d), view, view, beside)
            send(("s", k, 0, d), view, view, sibling)

    def from_y(k):
        for d in range(n_hi):
            view = rows_all.at[k, rows_of(hi_less(d), 1 - lo, b)]
            arrive(("y", k, d), view, beside)
            send(("s", k, 1, d), view, view, sibling)

    def from_sibling(k):
        for side in range(2):
            for d in range(n_hi):
                at = lo if side == 0 else 1 - lo
                view = rows_all.at[k, rows_of(hi_less(d), at, 1 - b)]
                arrive(("s", k, side, d), view, sibling)

    from_z(0)
    arrive("tok", whole.at[my_tok, other_cols], across)
    view = whole.at[my_tok, other_cols]
    send("tok2", view, view, sibling)
    from_y(0)
    from_z(1)

    arrive("tok2", whole.at[its_tok, other_cols], sibling)
    load_lin.wait()
    t_l = tile_of(ffl, 256)

    @pl.loop(0, ffl // t_l)
    def _(i):
        cols = pl.ds(pl.multiple_of(i * t_l, t_l), t_l)
        l_hidden[:, cols] = gelu_tanh(dot(whole[...], w_lin[:, cols])).astype(BF16)

    load_lout.wait()
    t_o = tile_of(half_d, 512)

    @pl.loop(0, half_d // t_o)
    def _(i):
        cols = pl.ds(pl.multiple_of(i * t_o, t_o), t_o)
        there = pl.ds(pl.multiple_of((1 - b) * half_d + i * t_o, t_o), t_o)
        l_send[:, cols] = dot(l_hidden[...], w_lout[:, there]).astype(BF16)

    send("l", l_send, l_recv, sibling)

    @pl.loop(0, half_d // t_o)
    def _(i):
        cols = pl.ds(pl.multiple_of(i * t_o, t_o), t_o)
        here = pl.ds(pl.multiple_of(b * half_d + i * t_o, t_o), t_o)
        l_own[:, cols] = dot(l_hidden[...], w_lout[:, here])

    from_sibling(0)
    load_hin.wait()
    t_h = tile_of(ffh, 256)
    t_r = tile_of(total_rows, 256)

    @pl.loop(0, total_rows // t_r)
    def _(j):
        rows = pl.ds(pl.multiple_of(j * t_r, t_r), t_r)

        @pl.loop(0, ffh // t_h)
        def _(i):
            cols = pl.ds(pl.multiple_of(i * t_h, t_h), t_h)
            value, rate = gelu_both(dot(rows_all[0, rows, :], w_hin[:, cols]))
            hidden[rows, cols] = value.astype(BF16)
            h_slope[rows, cols] = rate

    load_hout.wait()

    @pl.loop(0, total_rows // t_r)
    def _(j):
        rows = pl.ds(pl.multiple_of(j * t_r, t_r), t_r)

        @pl.loop(0, half_d // t_o)
        def _(i):
            cols = pl.ds(pl.multiple_of(i * t_o, t_o), t_o)
            there = pl.ds(pl.multiple_of((1 - b) * half_d + i * t_o, t_o), t_o)
            h_send[rows, cols] = dot(hidden[rows, :], w_hout[:, there]).astype(BF16)

    send("h", h_send, h_recv, sibling)

    @pl.loop(0, total_rows // t_r)
    def _(j):
        rows = pl.ds(pl.multiple_of(j * t_r, t_r), t_r)

        @pl.loop(0, half_d // t_o)
        def _(i):
            cols = pl.ds(pl.multiple_of(i * t_o, t_o), t_o)
            here = pl.ds(pl.multiple_of(b * half_d + i * t_o, t_o), t_o)
            h_own[rows, cols] = dot(hidden[rows, :], w_hout[:, here])

    arrive("h", h_recv, sibling)

    def shard_rows(hi_at, lo_at):
        return pl.ds(pl.multiple_of((hi_at * 2 + lo_at) * cap, cap), cap)

    for d in range(n_hi):
        at = hi_plus((d + 1) % n_hi)
        rows = shard_rows(at, 1 - lo)
        y_send[d] = (h_own[rows, :] + h_recv[rows, :].astype(F32)).astype(BF16)
        send(("hy", d), y_send.at[d], y_recv.at[d], beside)

    my_out = pl.ds(pl.multiple_of(m * out_w, out_w), out_w)
    its_out = pl.ds(pl.multiple_of((1 - m) * out_w, out_w), out_w)
    arrive("l", l_recv, sibling)
    l_xsend[...] = (l_own[:, its_out] + l_recv[:, its_out].astype(F32)).astype(BF16)
    send("lx", l_xsend, l_xrecv, across)

    from_y(1)
    kept = None
    for d in range(n_hi):
        step = (d + 1) % n_hi
        rows = shard_rows(hi_plus(step), lo)
        arrive(("hy", d), y_recv.at[d], beside)
        total = h_own[rows, :] + h_recv[rows, :].astype(F32) + y_recv[d].astype(F32)
        if step:
            z_send[step - 1] = total.astype(BF16)
            send(
                ("hz", step),
                z_send.at[step - 1],
                z_recv.at[step - 1],
                {"seq": hi_plus(step) * 2 + lo},
            )
        else:
            h_own[rows, :] = total

    from_sibling(1)
    store_rows = pltpu.make_async_copy(rows_all, rows_out, local_sem.at[len(local)])
    store_rows.start()

    @pl.loop(0, total_rows // t_r)
    def _(j):
        rows = pl.ds(pl.multiple_of(j * t_r, t_r), t_r)

        @pl.loop(0, ffh // t_h)
        def _(i):
            cols = pl.ds(pl.multiple_of(i * t_h, t_h), t_h)
            back = over_cols(rows_all[1, rows, :], w_hout[cols, :])
            slope[rows, cols] = (back * h_slope[rows, cols]).astype(BF16)

    home = shard_rows(hi, lo)
    for d in range(1, n_hi):
        arrive(("hz", d), z_recv.at[d - 1], {"seq": hi_less(d) * 2 + lo})
        h_own[home, :] = h_own[home, :] + z_recv[d - 1].astype(F32)
    x_send[...] = h_own[home, its_out].astype(BF16)
    send("hx", x_send, x_recv, across)
    arrive("lx", l_xrecv, across)
    arrive("hx", x_recv, across)

    share = (h_own[home, my_out] + x_recv[...].astype(F32)) * column_of(scale_row, 0, cap)
    coarse = share.astype(BF16)
    fine = (share - coarse.astype(F32)).astype(BF16)
    place = jnp.where(
        lax.broadcasted_iota(jnp.int32, (tok, cap), 0).astype(F32) == names, 1.0, 0.0
    ).astype(BF16)
    light = l_own[:, my_out] + l_recv[:, my_out].astype(F32) + l_xrecv[...].astype(F32)
    mixed[...] = (light + dot(place, coarse) + dot(place, fine)).astype(BF16)

    store_rows.wait()
    for copy in sends:
        copy.wait_send()


def per_device(
    n_seq,
    tokens,
    light_in,
    light_out,
    heavy_in,
    heavy_out,
    route_index,
    route_count,
    route_gate,
    cotangent,
):
    tok, half_d = tokens.shape
    width = 2 * half_d
    ffl = light_in.shape[1]
    ffh = heavy_in.shape[1]
    cap = route_index.shape[1]
    n_hi = n_seq // 2
    total_rows = n_seq * cap
    out_w = width // 4
    n_sem = 8 + 10 * n_hi
    vmem = pl.BlockSpec(memory_space=pltpu.VMEM)
    smem = pl.BlockSpec(memory_space=pltpu.SMEM)
    hbm = pl.BlockSpec(memory_space=pl.ANY)
    mixed, rows, hidden, slope = pl.pallas_call(
        functools.partial(kernel, n_seq, (tok, half_d, ffl, ffh, cap)),
        out_shape=(
            jax.ShapeDtypeStruct((tok, out_w), BF16),
            jax.ShapeDtypeStruct((2, total_rows, width), BF16),
            jax.ShapeDtypeStruct((total_rows, ffh), BF16),
            jax.ShapeDtypeStruct((total_rows, ffh), BF16),
        ),
        in_specs=[hbm, hbm, hbm, hbm, hbm, vmem, smem, vmem, hbm],
        out_specs=(vmem, hbm, vmem, vmem),
        scratch_shapes=[
            pltpu.VMEM((tok, width), BF16),
            pltpu.VMEM((tok, half_d), BF16),
            pltpu.VMEM(light_in.shape, BF16),
            pltpu.VMEM(light_out.shape, BF16),
            pltpu.VMEM(heavy_in.shape, BF16),
            pltpu.VMEM(heavy_out.shape, BF16),
            pltpu.VMEM((2, total_rows, width), BF16),
            pltpu.VMEM((tok, ffl), BF16),
            pltpu.VMEM((tok, half_d), F32),
            pltpu.VMEM((tok, half_d), BF16),
            pltpu.VMEM((tok, half_d), BF16),
            pltpu.VMEM((tok, out_w), BF16),
            pltpu.VMEM((tok, out_w), BF16),
            pltpu.VMEM((total_rows, ffh), F32),
            pltpu.VMEM((total_rows, half_d), F32),
            pltpu.VMEM((total_rows, half_d), BF16),
            pltpu.VMEM((total_rows, half_d), BF16),
            pltpu.VMEM((n_hi, cap, half_d), BF16),
            pltpu.VMEM((n_hi, cap, half_d), BF16),
            pltpu.VMEM((n_hi - 1, cap, half_d), BF16),
            pltpu.VMEM((n_hi - 1, cap, half_d), BF16),
            pltpu.VMEM((cap, out_w), BF16),
            pltpu.VMEM((cap, out_w), BF16),
            pltpu.SemaphoreType.DMA((8,)),
            pltpu.SemaphoreType.DMA((n_sem,)),
            pltpu.SemaphoreType.DMA((n_sem,)),
        ],
        compiler_params=pltpu.CompilerParams(
            collective_id=0, has_side_effects=True, vmem_limit_bytes=60 * 1024 * 1024
        ),
    )(
        tokens,
        light_in,
        light_out,
        heavy_in,
        heavy_out,
        route_index,
        route_count,
        route_gate,
        cotangent,
    )
    grad_out = over_rows(hidden, rows[1]).astype(BF16)
    grad_in = over_rows(rows[0], slope).astype(BF16)
    return mixed, grad_in, grad_out


def solution(mesh):
    in_specs = (
        P("seq", "mp"),
        P(None, ("branch", "mp")),
        P(("branch", "mp"), None),
        P(None, ("branch", "seq", "mp")),
        P(("branch", "seq", "mp"), None),
        P("seq", None),
        P("seq"),
        P("seq", None),
        P("seq", "mp"),
    )
    out_specs = (
        P("seq", ("branch", "mp")),
        P(None, ("branch", "seq", "mp")),
        P(("branch", "seq", "mp"), None),
    )
    return jax.shard_map(
        functools.partial(per_device, mesh.shape["seq"]),
        mesh=mesh,
        in_specs=in_specs,
        out_specs=out_specs,
        check_vma=False,
    )
```

time: 227 us -> 75.8 us (0.33)
  waiting for transfers between devices: 157 us -> 0 us
  Pallas kernels: 0 us -> 64.8 us
  matrix products: 28.6 us -> 8.34 us
  between operations: 15.9 us -> 1.31 us
  blocking collectives: 12.9 us -> 0 us
  other arithmetic: 7.14 us -> 0 us
  local copies, waits for them, and re-layouts: 4.22 us -> 0.81 us
    reduce_scatter x3 -> x0, waiting for transfers between devices: 94.4 us -> none  [the longest x1 59.5 us: per_device(): lax.psum_scatter(partial_terms.astype(jnp.bfloat16), 'seq', scatter_dimen...]
    pallas_call x0 -> x1, Pallas kernels: none -> 64.8 us  [per_device(): pl.pallas_call(functools.partial(kernel, n_seq, (tok, half_d, ffl, ffh, c...]
    all_gather x3 -> x0, waiting for transfers between devices: 62.2 us -> none  [the longest x1 50.9 us: per_device(): lax.all_gather(picked, 'seq', axis=0, tiled=True)]
    dot_general x3 -> x0, matrix products: 15.4 us -> none  [the longest x1 8.55 us: per_device(): jnp.dot(light_hidden, light_out, preferred_element_type=jnp.float32)]
    all_gather x2 -> x0, blocking collectives: 12.9 us -> none  [the longest x1 7.19 us: per_device(): lax.all_gather(picked, 'mp', axis=1, tiled=True)]
    dot_general x2, matrix products: 13.2 us -> 8.34 us  [over_rows(): lax.dot_general(left, right, (((0,), (0,)), ((), ())), preferred_element_...]
    scatter-add x1 -> x0, other arithmetic: 3.45 us -> none  [per_device(): mixed = light_share.at[positions].add(heavy_share).astype(jnp.bfloat16)]
    gather x2 -> x0, local copies, waits for them, and re-layouts: 2.78 us -> none  [the longest x1 2.13 us: per_device(): picked = jnp.take(tokens, positions, axis=0)]
  transfers between devices with their start and end apart: 6 -> 0, of which waited for: 4 -> 0; matrix products, arithmetic and copies ran while one was open for 10% -> 0% of each run, Pallas kernels for 0% -> 0%
where the time goes in v1:
time: 75.8 us; the launch traced here: 75.3 us
  Pallas kernels  64.8 us (85%)
  matrix products  8.34 us (11%)
  between operations  1.31 us (2%)
  local copies, waits for them, and re-layouts  0.81 us (1%)
    pallas_call x1, Pallas kernels, per_device(): pl.pallas_call(functools.partial(kernel, n_seq, (tok, half_d, ffl, ffh, c...  64.8 us
    dot_general x2, matrix products, over_rows(): lax.dot_general(left, right, (((0,), (0,)), ((), ())), preferred_element_...  8.34 us

profile of v1, /device:TPU:0, one launch (start us, length us, event | category | flops | bytes accessed | tf_op | source)
XLA Modules:
  0.0 75.3 jit_solution(17139199885286856232)
XLA Ops:
  1.3 64.8 %shard_map.112 = (bf16[256,1024]{1,0:T(8,128)(2,1)}, bf16[2,256,4096]{2,1,0:T(8,128)(2,1)}, bf16[256,512]{1,0:T(8,128)(2,1)}, bf16[256,512]{1,0:T(8,128)(2,1)}) custom-call(bf16[256,2048]{1,0:T(8,128)(2,1)} %tokens.1, bf16[4096,512]{1,0:T(8,128)(2,1)} %light_in.1, bf16[512,4096]{1,0:T(8,128)(2,1)} %light_out.1, bf16[4096,512]{1,0:T(8,128)(2,1)} %heavy_in.1, ...), custom_call_target="tpu_custom_call" | custom-call | tf_op jit(solution)/shard_map/pallas_call | solution.py:397
  66.1 0.0 copy-start
  66.1 0.0 copy-start.2
  66.1 5.0 %convolution_convert_fusion.1 = bf16[4096,512]{1,0:T(8,128)(2,1)} fusion(bf16[256,512]{1,0:T(8,128)(2,1)} %get-tuple-element.9, bf16[2,256,4096]{2,1,0:T(8,128)(2,1)} %get-tuple-element.8), kind=kOutput, calls=%fused_computation.1 | convolution fusion | flops 1075838976 | bytes 6553600 | tf_op jit(solution)/shard_map/dot_general | solution.py:32
  71.2 0.0 copy-done
  71.2 0.0 copy-done.2
  71.2 0.0 copy-start.1
  71.2 3.3 %convolution_convert_fusion = bf16[512,4096]{1,0:T(8,128)(2,1)} fusion(bf16[256,512]{1,0:T(8,128)(2,1)S(1)} %copy-done.2, bf16[2,256,4096]{2,1,0:T(8,128)(2,1)S(1)} %copy-done), kind=kOutput, calls=%fused_computation | convolution fusion | flops 1075838976 | bytes 6553600 | tf_op jit(solution)/shard_map/dot_general | solution.py:32
  74.5 0.0 copy-done.1
  74.5 0.8 %copy.14 = bf16[256,1024]{1,0:T(8,128)(2,1)} copy(bf16[256,1024]{1,0:T(8,128)(2,1)S(1)} %copy-done.1) | data formatting | bytes 1048576
Async XLA Ops:
  66.1 5.1 %copy-start = (bf16[2,256,4096]{2,1,0:T(8,128)(2,1)S(1)}, bf16[2,256,4096]{2,1,0:T(8,128)(2,1)}, u32[]{:S(2)}) copy-start(bf16[2,256,4096]{2,1,0:T(8,128)(2,1)} %get-tuple-element.8) | copy-start | bytes 12582916
  66.1 5.1 %copy-start.2 = (bf16[256,512]{1,0:T(8,128)(2,1)S(1)}, bf16[256,512]{1,0:T(8,128)(2,1)}, u32[]{:S(2)}) copy-start(bf16[256,512]{1,0:T(8,128)(2,1)} %get-tuple-element.10) | copy-start | bytes 786436
  71.2 3.3 %copy-start.1 = (bf16[256,1024]{1,0:T(8,128)(2,1)S(1)}, bf16[256,1024]{1,0:T(8,128)(2,1)}, u32[]{:S(2)}) copy-start(bf16[256,1024]{1,0:T(8,128)(2,1)} %get-tuple-element.14) | copy-start | bytes 1572868

commit v2 on v1

--- a/solution.py
+++ b/solution.py
@@ -197,7 +197,7 @@
     its_tok = pl.ds(pl.multiple_of((1 - b) * tok_half, tok_half), tok_half)
     send("tok", tokens.at[my_tok], whole.at[my_tok, own_cols], across)
 
-    for k in range(2):
+    def begin(k):
         arrive(("x", k), rows_all.at[k, mine, other_cols], across)
         view = rows_all.at[k, mine]
         for d in range(1, n_hi):
@@ -225,12 +225,12 @@
                 view = rows_all.at[k, rows_of(hi_less(d), at, 1 - b)]
                 arrive(("s", k, side, d), view, sibling)
 
+    begin(0)
     from_z(0)
+    begin(1)
     arrive("tok", whole.at[my_tok, other_cols], across)
     view = whole.at[my_tok, other_cols]
     send("tok2", view, view, sibling)
-    from_y(0)
-    from_z(1)
 
     arrive("tok2", whole.at[its_tok, other_cols], sibling)
     load_lin.wait()
@@ -251,6 +251,8 @@
         l_send[:, cols] = dot(l_hidden[...], w_lout[:, there]).astype(BF16)
 
     send("l", l_send, l_recv, sibling)
+    from_z(1)
+    from_y(0)
 
     @pl.loop(0, half_d // t_o)
     def _(i):
@@ -368,6 +370,11 @@
     store_rows.wait()
     for copy in sends:
         copy.wait_send()
+
+
+def grad_kernel(rows, hidden, slope, grad_in, grad_out):
+    grad_in[...] = over_rows(rows[0], slope[...]).astype(BF16)
+    grad_out[...] = over_rows(hidden[...], rows[1]).astype(BF16)
 
 
 def per_device(
@@ -446,8 +453,25 @@
         route_gate,
         cotangent,
     )
-    grad_out = over_rows(hidden, rows[1]).astype(BF16)
-    grad_in = over_rows(rows[0], slope).astype(BF16)
+    tile = tile_of(width, 512)
+    grad_in, grad_out = pl.pallas_call(
+        grad_kernel,
+        grid=(width // tile,),
+        out_shape=(
+            jax.ShapeDtypeStruct((width, ffh), BF16),
+            jax.ShapeDtypeStruct((ffh, width), BF16),
+        ),
+        in_specs=[
+            pl.BlockSpec((2, total_rows, tile), lambda i: (0, 0, i)),
+            pl.BlockSpec((total_rows, ffh), lambda i: (0, 0)),
+            pl.BlockSpec((total_rows, ffh), lambda i: (0, 0)),
+        ],
+        out_specs=(
+            pl.BlockSpec((tile, ffh), lambda i: (i, 0)),
+            pl.BlockSpec((ffh, tile), lambda i: (0, i)),
+        ),
+        compiler_params=pltpu.CompilerParams(vmem_limit_bytes=60 * 1024 * 1024),
+    )(rows, hidden, slope)
     return mixed, grad_in, grad_out
 
 

time: 75.8 us -> 73.2 us (0.966)
  matrix products: 8.34 us -> 0 us
  Pallas kernels: 64.8 us -> 70.8 us
    pallas_call x0 -> x1, Pallas kernels: none -> 8.54 us  [per_device(): pl.pallas_call(grad_kernel, grid=(width // tile,), out_shape=(jax.ShapeDt...]
    dot_general x2 -> x0, matrix products: 8.34 us -> none  [over_rows(): lax.dot_general(left, right, (((0,), (0,)), ((), ())), preferred_element_...]
    pallas_call x1, Pallas kernels: 64.8 us -> 62.2 us  [per_device(): pl.pallas_call(functools.partial(kernel, n_seq, (tok, half_d, ffl, ffh, c...]
where the time goes in v2:
time: 73.2 us; the launch traced here: 72.9 us
  Pallas kernels  70.8 us (97%)
  between operations  1.3 us (2%)
  local copies, waits for them, and re-layouts  0.8 us (1%)
    pallas_call x1, Pallas kernels, per_device(): pl.pallas_call(functools.partial(kernel, n_seq, (tok, half_d, ffl, ffh, c...  62.2 us
    pallas_call x1, Pallas kernels, per_device(): pl.pallas_call(grad_kernel, grid=(width // tile,), out_shape=(jax.ShapeDt...  8.54 us

profile of v2, /device:TPU:0, one launch (start us, length us, event | category | flops | bytes accessed | tf_op | source)
XLA Modules:
  0.0 72.9 jit_solution(10599036143022293294)
XLA Ops:
  1.3 62.2 %shard_map.112 = (bf16[256,1024]{1,0:T(8,128)(2,1)}, bf16[2,256,4096]{2,1,0:T(8,128)(2,1)}, bf16[256,512]{1,0:T(8,128)(2,1)}, bf16[256,512]{1,0:T(8,128)(2,1)}) custom-call(bf16[256,2048]{1,0:T(8,128)(2,1)} %tokens.1, bf16[4096,512]{1,0:T(8,128)(2,1)} %light_in.1, bf16[512,4096]{1,0:T(8,128)(2,1)} %light_out.1, bf16[4096,512]{1,0:T(8,128)(2,1)} %heavy_in.1, ...), custom_call_target="tpu_custom_call" | custom-call | tf_op jit(solution)/shard_map/pallas_call | solution.py:404
  63.5 0.0 copy-start
  63.5 8.5 %shard_map.113 = (bf16[4096,512]{1,0:T(8,128)(2,1)}, bf16[512,4096]{1,0:T(8,128)(2,1)}) custom-call(bf16[2,256,4096]{2,1,0:T(8,128)(2,1)} %get-tuple-element.10.rows, bf16[256,512]{1,0:T(8,128)(2,1)} %get-tuple-element.11.hidden, bf16[256,512]{1,0:T(8,128)(2,1)} %get-tuple-element.12.slope), custom_call_target="tpu_custom_call" | custom-call | tf_op jit(solution)/shard_map/pallas_call | solution.py:457
  72.1 0.0 copy-done
  72.1 0.8 %copy.14 = bf16[256,1024]{1,0:T(8,128)(2,1)} copy(bf16[256,1024]{1,0:T(8,128)(2,1)S(1)} %copy-done) | data formatting | bytes 1048576
Async XLA Ops:
  63.5 8.6 %copy-start = (bf16[256,1024]{1,0:T(8,128)(2,1)S(1)}, bf16[256,1024]{1,0:T(8,128)(2,1)}, u32[]{:S(2)}) copy-start(bf16[256,1024]{1,0:T(8,128)(2,1)} %get-tuple-element.18) | copy-start | bytes 1572868
